TPU v7x, 256 devices: a whole 4x4x8 slice. The times are simulated.
256 devices in a mesh: row: 8 (over y, z_lo), col: 4 (over z_hi), layer: 8 (over x, core).
Axes of the slice: x: 4, y: 4, z: 8 (z_hi: 4, z_lo: 2; z = z_hi * 2 + z_lo), core: 2. Of those that a mesh axis runs over, the one named last changes fastest.
Arguments:
- density: bfloat16 [512, 8, 128, 128], P(('row', 'col')), may hold values from -1.1953125 to 1.1953125
- tile_cols: int32 [512, 8], replicated, may hold values from 0 to 511, as said below
- out_cols: int32 [512, 8, 4], P(('row', 'col')), may hold values from 0 to 511, as said below
Outputs:
- purified: bfloat16 [512, 8, 4, 128, 128], P(('row', 'col'), 'layer')
Inputs may be any that keep to these rules, and one draw needn't show every extreme that they name: Column set l holds the block columns c with (c // 2) % 8 == l; tile_cols[i, l] lies in column set l, so a block row has exactly one tile in each column set. For each i and l, the 4 block columns out_cols[i, l, :] are distinct and lie in column set l.
All inputs are finite; a program needn't handle non-finite values.
Results may differ from a plain program's by a relative error of at most 0.0044.
Values may be sent and summed in bfloat16 or wider, within the bound.
No kernel may reach another device: no remote copies, remote signals or barrier semaphores. Data moves between devices by JAX's collectives and lax.ppermute only.
A program may use at most 128 MiB of HBM per device.

v0:
```python
import jax
import jax.numpy as jnp
from jax import lax
from jax.sharding import PartitionSpec as P


def filtered_product(left_tiles, index_tiles, column, colset, wanted):
    step_rows = 4
    row_total = left_tiles.shape[0]
    slot_count = wanted.shape[1]

    def row_block(first_row):
        left_part = lax.dynamic_slice_in_dim(left_tiles, first_row, step_rows, 0)
        index_part = lax.dynamic_slice_in_dim(index_tiles, first_row, step_rows, 0)
        wanted_part = lax.dynamic_slice_in_dim(wanted, first_row, step_rows, 0)
        b_tiles = jnp.take(column, index_part, axis=0)
        products = jnp.einsum(
            "imab,imbc->imac", left_part, b_tiles, preferred_element_type=jnp.float32
        )
        reached = jnp.take(colset, index_part, axis=0)
        picked = []
        for slot in range(slot_count):
            matches = reached == wanted_part[:, slot][:, None]
            picked.append(jnp.sum(jnp.where(matches[:, :, None, None], products, 0.0), axis=1))
        return jnp.stack(picked, axis=1)

    starts = jnp.arange(row_total // step_rows, dtype=jnp.int32) * step_rows
    blocks = lax.map(row_block, starts)
    return blocks.reshape((row_total,) + blocks.shape[2:])


def on_device(density, tile_cols, out_cols):
    own_rows = density.shape[0]
    tile_size = density.shape[2]
    layer_index = lax.axis_index("layer")
    group_index = lax.axis_index(("row", "col"))
    own_slot = lax.dynamic_index_in_dim(density, layer_index, 1, keepdims=False)
    column = lax.all_gather(own_slot, ("row", "col"), axis=0, tiled=True)
    colset = lax.dynamic_index_in_dim(tile_cols, layer_index, 1, keepdims=False)
    own_cols = lax.dynamic_slice_in_dim(tile_cols, group_index * own_rows, own_rows, 0)
    wanted = lax.dynamic_index_in_dim(out_cols, layer_index, 1, keepdims=False)
    square = filtered_product(density, own_cols, column, colset, wanted)
    square_low = square.astype(jnp.bfloat16)
    square_all = lax.all_gather(square_low[:, None], "layer", axis=1, tiled=True)
    slot_total = square_all.shape[1] * square_all.shape[2]
    cube = filtered_product(
        square_all.reshape(own_rows, slot_total, tile_size, tile_size),
        out_cols.reshape(own_rows, slot_total),
        column,
        colset,
        wanted,
    )
    purified = (3.0 * square - 2.0 * cube).astype(jnp.bfloat16)
    return purified[:, None]


def solution(mesh):
    placed = (P(("row", "col"), None, None, None), P(), P(("row", "col"), None, None))
    return jax.shard_map(
        on_device,
        mesh=mesh,
        in_specs=placed,
        out_specs=P(("row", "col"), "layer", None, None, None),
        check_vma=False,
    )
```

profile of v0, /device:TPU:1, one launch (start us, length us, event | category | flops | bytes accessed | tf_op | source)
XLA Modules:
  0.0 619.5 jit_solution(7918923848924142683)
XLA Ops:
  6.5 1.9 constant_dynamic-slice_fusion.2
  8.7 0.7 dynamic-slice_bitcast_fusion
  9.4 369.9 %all-gather.6.cloned.1.call-done = bf16[512,1,128,128]{3,2,1,0:T(8,128)(2,1)} async-done(((bf16[16,1,128,128]{3,2,1,0:T(8,128)(2,1)}), bf16[512,1,128,128]{3,2,1,0:T(8,128)(2,1)}) %all-gather.6.cloned.1.call-update) | async-done | bytes 16777232 | tf_op jit(solution)/shard_map/all_gather | solution.py:38
  379.3 2.5 broadcast.88.clone
  381.8 54.0 %while.20 = (s32[]{:T(128)}, f32[4,4,4,128,128]{4,3,2,1,0:T(8,128)}, s32[4]{0:T(128)S(1)}, s32[16,8]{1,0:T(8,128)S(1)}, s32[512]{0:T(512)S(1)}, /*index=5*/s32[1...) while((s32[]{:T(128)}, ...), condition=%wide.region_5.6_spmd, body=%wide.region_0.5_spmd.sunk | while | flops 139462112 | bytes 7347275 | solution.py:28
  381.8 0.6 dynamic_slice.78
  384.4 0.7 gather_fusion
  385.4 6.5 %gather_fusion.1 = bf16[32,128,128]{2,1,0:T(8,128)(2,1)S(1)} fusion(bf16[512,128,128]{2,1,0:T(8,128)(2,1)} %get-tuple-element.344, s32[1024]{0:T(1024)S(1)} %pad_clamp_fusion.4), kind=kCustom, calls=%fused_computation.1.clone.1 | custom fusion | bytes 2097280 | tf_op jit(solution)/shard_map/while/body/eval_jaxpr/jit(_take)/gather | solution.py:16
  392.0 2.2 select_reduce_fusion.10
  394.2 1.1 fusion.18
  395.2 0.6 dynamic_slice.78
  397.9 0.7 gather_fusion
  398.9 6.5 %gather_fusion.1 = bf16[32,128,128]{2,1,0:T(8,128)(2,1)S(1)} fusion(bf16[512,128,128]{2,1,0:T(8,128)(2,1)} %get-tuple-element.344, s32[1024]{0:T(1024)S(1)} %pad_clamp_fusion.4), kind=kCustom, calls=%fused_computation.1.clone.1 | custom fusion | bytes 2097280 | tf_op jit(solution)/shard_map/while/body/eval_jaxpr/jit(_take)/gather | solution.py:16
  405.4 2.2 select_reduce_fusion.10
  407.7 1.0 fusion.18
  408.7 0.6 dynamic_slice.78
  411.4 0.7 gather_fusion
  412.4 6.5 %gather_fusion.1 = bf16[32,128,128]{2,1,0:T(8,128)(2,1)S(1)} fusion(bf16[512,128,128]{2,1,0:T(8,128)(2,1)} %get-tuple-element.344, s32[1024]{0:T(1024)S(1)} %pad_clamp_fusion.4), kind=kCustom, calls=%fused_computation.1.clone.1 | custom fusion | bytes 2097280 | tf_op jit(solution)/shard_map/while/body/eval_jaxpr/jit(_take)/gather | solution.py:16
  418.9 2.2 select_reduce_fusion.10
  421.2 1.1 fusion.18
  422.2 0.6 dynamic_slice.78
  424.9 0.7 gather_fusion
  425.9 6.5 %gather_fusion.1 = bf16[32,128,128]{2,1,0:T(8,128)(2,1)S(1)} fusion(bf16[512,128,128]{2,1,0:T(8,128)(2,1)} %get-tuple-element.344, s32[1024]{0:T(1024)S(1)} %pad_clamp_fusion.4), kind=kCustom, calls=%fused_computation.1.clone.1 | custom fusion | bytes 2097280 | tf_op jit(solution)/shard_map/while/body/eval_jaxpr/jit(_take)/gather | solution.py:16
  432.4 2.2 select_reduce_fusion.10
  434.7 1.1 fusion.18
  435.7 3.9 convert_element_type.26
  439.7 85.0 %all-gather.4.cloned.1.call-done = bf16[16,8,4,128,128]{4,3,2,1,0:T(8,128)(2,1)} async-done(((bf16[16,1,4,128,128]{4,3,2,1,0:T(8,128)(2,1)}), bf16[16,8,4,128,128]{4,3,2,1,0:T(8,128)(2,1)}) %all-gather.4.cloned.1.call-update) | async-done | bytes 16777232 | tf_op jit(solution)/shard_map/all_gather | solution.py:44
  524.8 2.6 broadcast.88
  527.3 79.6 %while.21 = (s32[]{:T(128)}, f32[4,4,4,128,128]{4,3,2,1,0:T(8,128)}, s32[4]{0:T(128)S(1)}, s32[16,32]{1,0:T(8,128)S(1)}, s32[512]{0:T(512)S(1)}, /*index=5*/s32[...) while((s32[]{:T(128)}, ...), condition=%wide.region_11.12_spmd, body=%wide.region_6.11_spmd.sunk | while | flops 556272512 | bytes 19936620 | solution.py:28
  527.3 0.6 dynamic_slice.83
  530.0 1.3 gather_fusion.2
  531.5 8.8 %gather_fusion.3 = bf16[128,128,128]{2,1,0:T(8,128)(2,1)} fusion(bf16[512,128,128]{2,1,0:T(8,128)(2,1)} %get-tuple-element.377, s32[1024]{0:T(1024)S(1)} %pad_clamp_fusion.5), kind=kCustom, calls=%fused_computation.3.clone.1 | custom fusion | bytes 8389120 | tf_op jit(solution)/shard_map/while/body/eval_jaxpr/jit(_take)/gather | solution.py:16
  540.3 5.8 select_reduce_fusion.11
  546.1 1.1 fusion.19
  547.2 0.6 dynamic_slice.83
  549.8 1.3 gather_fusion.2
  551.4 8.8 %gather_fusion.3 = bf16[128,128,128]{2,1,0:T(8,128)(2,1)} fusion(bf16[512,128,128]{2,1,0:T(8,128)(2,1)} %get-tuple-element.377, s32[1024]{0:T(1024)S(1)} %pad_clamp_fusion.5), kind=kCustom, calls=%fused_computation.3.clone.1 | custom fusion | bytes 8389120 | tf_op jit(solution)/shard_map/while/body/eval_jaxpr/jit(_take)/gather | solution.py:16
  560.2 5.8 select_reduce_fusion.11
  566.0 1.1 fusion.19
  569.7 1.3 gather_fusion.2
  571.3 8.8 %gather_fusion.3 = bf16[128,128,128]{2,1,0:T(8,128)(2,1)} fusion(bf16[512,128,128]{2,1,0:T(8,128)(2,1)} %get-tuple-element.377, s32[1024]{0:T(1024)S(1)} %pad_clamp_fusion.5), kind=kCustom, calls=%fused_computation.3.clone.1 | custom fusion | bytes 8389120 | tf_op jit(solution)/shard_map/while/body/eval_jaxpr/jit(_take)/gather | solution.py:16
  580.1 5.8 select_reduce_fusion.11
  585.9 1.1 fusion.19
  589.6 1.3 gather_fusion.2
  591.2 8.8 %gather_fusion.3 = bf16[128,128,128]{2,1,0:T(8,128)(2,1)} fusion(bf16[512,128,128]{2,1,0:T(8,128)(2,1)} %get-tuple-element.377, s32[1024]{0:T(1024)S(1)} %pad_clamp_fusion.5), kind=kCustom, calls=%fused_computation.3.clone.1 | custom fusion | bytes 8389120 | tf_op jit(solution)/shard_map/while/body/eval_jaxpr/jit(_take)/gather | solution.py:16
  600.0 5.8 select_reduce_fusion.11
  605.8 1.1 fusion.19
  606.9 5.7 subtract_convert_fusion
  (79 shorter events, 4.8 us)
Async XLA Ops:
  6.5 2.0 copy-start
  6.5 372.8 %all-gather.6.cloned.1.call-start = ((), (), s32[]{:S(2)}) async-start(), calls=%async_computation.1 | async-start | bytes 17301504 | tf_op jit(solution)/shard_map/all_gather | solution.py:38
  8.5 516.3 %all-gather.4.cloned.1.call-start = ((), (), s32[]{:S(2)}) async-start(), calls=%async_computation | async-start | bytes 18874368 | tf_op jit(solution)/shard_map/all_gather | solution.py:44
  435.7 3.9 copy-start.1
Sparse Core Ops, SparseCore 0:
  9.1 370.1 all-gather.5
  439.8 84.9 all-gather.3
where the time goes:
time: 620 us; the launch traced here: 619 us
  waiting for transfers between devices  455 us (73%)
  local copies, waits for them, and re-layouts  83.5 us (13%)
  matrix products  32.2 us (5%)
  other arithmetic  19.6 us (3%)
  loops' own time  15.8 us (3%)
  between operations  13.4 us (2%)
    all_gather x1, waiting for transfers between devices, on_device(): column = lax.all_gather(own_slot, ('row', 'col'), axis=0, tiled=True)  370 us
    all_gather x1, waiting for transfers between devices, on_device(): lax.all_gather(square_low[:, None], 'layer', axis=1, tiled=True)  85 us
    gather x8, local copies, waits for them, and re-layouts, row_block(): b_tiles = jnp.take(column, index_part, axis=0)  61.1 us
    dot_general x8, matrix products, row_block(): jnp.einsum('imab,imbc->imac', left_part, b_tiles, preferred_element_type=...  32.2 us
    another operation x2, loops' own time, filtered_product(): blocks = lax.map(row_block, starts)  15.8 us
  transfers between devices with their start and end apart: 2, of which 2 were waited for; matrix products, arithmetic and copies ran while one was open for 0% of the time, Pallas kernels for 0%

commit v1 on v0

v1 whole, which is shorter than its diff:
```python
import jax
import jax.numpy as jnp
from jax import lax
from jax.experimental import pallas as pl
from jax.experimental.pallas import tpu as pltpu
from jax.sharding import Mesh
from jax.sharding import PartitionSpec as P

BATCH = 16
GROUP = 4
FIRST = 64
VMEM_LIMIT = 48 * 1024 * 1024


def square_kernel(jobs, count, left, right, square, square_low, left_buf, right_buf, total, left_sem, right_sem):
    outs = square.shape[0]
    batches = (count[0] + BATCH - 1) // BATCH
    total[...] = jnp.zeros_like(total)

    def start(batch):
        slot = lax.rem(batch, 2)
        for j in range(BATCH):
            word = jobs[batch * BATCH + j]
            pltpu.make_async_copy(left.at[(word >> 7) & 127], left_buf.at[slot, j], left_sem.at[slot]).start()
            pltpu.make_async_copy(right.at[word >> 14], right_buf.at[slot, j], right_sem.at[slot]).start()

    @pl.when(batches > 0)
    def _():
        start(0)

    def body(batch, carry):
        slot = lax.rem(batch, 2)

        @pl.when(batch + 1 < batches)
        def _():
            start(batch + 1)

        pltpu.make_async_copy(left_buf.at[slot], left_buf.at[slot], left_sem.at[slot]).wait()
        pltpu.make_async_copy(right_buf.at[slot], right_buf.at[slot], right_sem.at[slot]).wait()
        for first in range(0, BATCH, GROUP):
            products = [
                lax.dot_general(
                    right_buf[slot, j], left_buf[slot, j], (((1,), (1,)), ((), ())), preferred_element_type=jnp.float32
                )
                for j in range(first, first + GROUP)
            ]
            for j in range(GROUP):
                target = jobs[batch * BATCH + first + j] & 127
                total[target] += products[j]
        return carry

    lax.fori_loop(0, batches, body, 0)
    square[...] = total[:outs]
    square_low[...] = total[:outs].astype(jnp.bfloat16)


def square_part(jobs, count, left, right):
    part = right.shape[1]
    return pl.pallas_call(
        square_kernel,
        out_shape=(
            jax.ShapeDtypeStruct((64, part, 128), jnp.float32),
            jax.ShapeDtypeStruct((64, part, 128), jnp.bfloat16),
        ),
        in_specs=[
            pl.BlockSpec(memory_space=pltpu.SMEM),
            pl.BlockSpec(memory_space=pltpu.SMEM),
            pl.BlockSpec(memory_space=pl.ANY),
            pl.BlockSpec(memory_space=pl.ANY),
        ],
        out_specs=(pl.BlockSpec(memory_space=pltpu.VMEM), pl.BlockSpec(memory_space=pltpu.VMEM)),
        scratch_shapes=[
            pltpu.VMEM((2, BATCH, 128, 128), jnp.bfloat16),
            pltpu.VMEM((2, BATCH, part, 128), jnp.bfloat16),
            pltpu.VMEM((65, part, 128), jnp.float32),
            pltpu.SemaphoreType.DMA((2,)),
            pltpu.SemaphoreType.DMA((2,)),
        ],
        compiler_params=pltpu.CompilerParams(vmem_limit_bytes=VMEM_LIMIT),
        name="square_part",
    )(jobs, count, left, right)


def cube_kernel(*refs):
    jobs, count, right_a, right_b, square_a, square_b = refs[:6]
    pieces_a, pieces_b = refs[6:16], refs[16:26]
    out, right_buf, left_buf, total, right_sem, left_sem = refs[26:]
    first_part = square_a.shape[1]
    rest = 128 - first_part
    batches = (count[0] + BATCH - 1) // BATCH
    total[...] = jnp.zeros_like(total)

    def start(batch):
        slot = lax.rem(batch, 2)
        for j in range(BATCH):
            word = jobs[batch * BATCH + j]
            place = word >> 17
            piece = (word >> 13) & 15
            at = (word >> 7) & 63
            pltpu.make_async_copy(
                right_a.at[place], right_buf.at[slot, j, pl.ds(0, first_part)], right_sem.at[slot]
            ).start()
            pltpu.make_async_copy(
                right_b.at[place], right_buf.at[slot, j, pl.ds(first_part, rest)], right_sem.at[slot]
            ).start()
            for p in range(10):

                @pl.when(piece == p)
                def _(p=p, j=j, at=at):
                    pltpu.make_async_copy(
                        pieces_a[p].at[at], left_buf.at[slot, j, pl.ds(0, first_part)], left_sem.at[slot]
                    ).start()
                    pltpu.make_async_copy(
                        pieces_b[p].at[at], left_buf.at[slot, j, pl.ds(first_part, rest)], left_sem.at[slot]
                    ).start()

    @pl.when(batches > 0)
    def _():
        start(0)

    def body(batch, carry):
        slot = lax.rem(batch, 2)

        @pl.when(batch + 1 < batches)
        def _():
            start(batch + 1)

        pltpu.make_async_copy(right_buf.at[slot], right_buf.at[slot], right_sem.at[slot]).wait()
        pltpu.make_async_copy(left_buf.at[slot], left_buf.at[slot], left_sem.at[slot]).wait()
        for first in range(0, BATCH, GROUP):
            products = [
                jnp.dot(right_buf[slot, j], left_buf[slot, j], preferred_element_type=jnp.float32)
                for j in range(first, first + GROUP)
            ]
            for j in range(GROUP):
                target = jobs[batch * BATCH + first + j] & 127
                total[target] += products[j]
        return carry

    lax.fori_loop(0, batches, body, 0)

    def finish(step, carry):
        for j in range(GROUP):
            o = step * GROUP + j
            square = jnp.concatenate([square_a[o], square_b[o]], axis=0)
            out[o] = (3.0 * square - 2.0 * total[o]).T.astype(jnp.bfloat16)
        return carry

    lax.fori_loop(0, out.shape[0] // GROUP, finish, 0)


def cube_part(jobs, count, right_a, right_b, square_a, square_b, pieces_a, pieces_b):
    smem = pl.BlockSpec(memory_space=pltpu.SMEM)
    vmem = pl.BlockSpec(memory_space=pltpu.VMEM)
    anywhere = pl.BlockSpec(memory_space=pl.ANY)
    return pl.pallas_call(
        cube_kernel,
        out_shape=jax.ShapeDtypeStruct((64, 128, 128), jnp.bfloat16),
        in_specs=[smem, smem, anywhere, anywhere, vmem, vmem] + [anywhere] * 20,
        out_specs=vmem,
        scratch_shapes=[
            pltpu.VMEM((2, BATCH, 128, 128), jnp.bfloat16),
            pltpu.VMEM((2, BATCH, 128, 128), jnp.bfloat16),
            pltpu.VMEM((65, 128, 128), jnp.float32),
            pltpu.SemaphoreType.DMA((2,)),
            pltpu.SemaphoreType.DMA((2,)),
        ],
        compiler_params=pltpu.CompilerParams(vmem_limit_bytes=VMEM_LIMIT),
        name="cube_part",
    )(jobs, count, right_a, right_b, square_a, square_b, *pieces_a, *pieces_b)


def packed_jobs(matched, payload):
    total = matched.shape[0]
    ids = jnp.arange(total, dtype=jnp.int32)
    hits = matched.astype(jnp.int32)
    rank = jnp.sum(jnp.where(ids[None, :] < ids[:, None], hits[None, :], 0), axis=1)
    chosen = (rank[None, :] == ids[:, None]) & matched[None, :]
    words = jnp.sum(jnp.where(chosen, payload[None, :], 0), axis=1)
    count = jnp.sum(hits)
    return jnp.where(ids < count, words, 64).astype(jnp.int32), count[None]


def place_of(k):
    group, within = k // 16, k % 16
    y, z_lo, z_hi = group // 8, (group // 4) % 2, group % 4
    return ((y * 4 + z_hi) * 2 + z_lo) * 16 + within


def job_lists(tile_cols, out_cols, layer, group, x, core):
    own_rows = out_cols.shape[0]
    colset = lax.dynamic_index_in_dim(tile_cols, layer, 1, keepdims=False)
    own_cols = lax.dynamic_slice_in_dim(tile_cols, group * own_rows, own_rows, 0)
    wanted = lax.dynamic_index_in_dim(out_cols, layer, 1, keepdims=False)
    through = out_cols.reshape(own_rows, 32)
    every = jnp.arange(tile_cols.shape[0], dtype=jnp.int32)
    rows = jnp.arange(own_rows, dtype=jnp.int32)[:, None]

    def lookup(index):
        return jnp.sum(jnp.where(index[..., None] == every, colset, 0), axis=-1)

    def slots(index):
        same = lookup(index)[:, :, None] == wanted[:, None, :]
        slot = jnp.sum(jnp.where(same, jnp.arange(4, dtype=jnp.int32), 0), axis=-1)
        return jnp.any(same, axis=-1), rows * 4 + slot

    matched, target = slots(own_cols)
    source = rows * 8 + jnp.arange(8, dtype=jnp.int32)[None, :]
    words = (place_of(own_cols) << 14) | (source << 7) | target
    square_jobs = packed_jobs(matched.reshape(-1), words.reshape(-1))

    matched, target = slots(through)
    m = jnp.arange(32, dtype=jnp.int32)[None, :]
    u, t = m // 4, m % 4
    distance = (u // 2 - x) % 4
    half = rows // (own_rows // 2)
    piece = jnp.where(distance == 2, 3 + half, jnp.where(distance == 3, 1, jnp.where(distance == 1, 2, 0)))
    piece = piece + jnp.where(u % 2 == core, 0, 5)
    at = jnp.where(distance == 2, rows % (own_rows // 2), rows) * 4 + t
    words = (place_of(through) << 17) | (piece << 13) | (at << 7) | target
    cube_jobs = packed_jobs(matched.reshape(-1), words.reshape(-1))
    return square_jobs, cube_jobs


def spread(part):
    half = part.shape[0] // 2

    def along_x(block, step):
        return lax.ppermute(block, "x", [(i, (i + step) % 4) for i in range(4)])

    def to_other_core(block):
        return lax.ppermute(block, "core", [(0, 1), (1, 0)])

    below, above = along_x(part, 1), along_x(part, -1)
    far_a, far_b = along_x(below[:half], 1), along_x(above[half:], -1)
    mine = [part, below, above, far_a, far_b]
    return mine + [to_other_core(block) for block in mine]


def on_device(density, tile_cols, out_cols):
    x, core = lax.axis_index("x"), lax.axis_index("core")
    layer = x * 2 + core
    group = lax.axis_index(("y", "z_lo", "z_hi"))
    own_rows = density.shape[0]
    own = jnp.swapaxes(lax.dynamic_index_in_dim(density, layer, 1, keepdims=False), 1, 2)
    own_a, own_b = own[:, :FIRST], own[:, FIRST:]
    right_a = lax.all_gather(own_a, ("y", "z_hi", "z_lo"), axis=0, tiled=True)
    right_b = lax.all_gather(own_b, ("y", "z_hi", "z_lo"), axis=0, tiled=True)
    square_jobs, cube_jobs = job_lists(tile_cols, out_cols, layer, group, x, core)
    left = density.reshape(own_rows * 8, 128, 128)
    square_a, low_a = square_part(*square_jobs, left, right_a)
    pieces_a = spread(low_a)
    square_b, low_b = square_part(*square_jobs, left, right_b)
    pieces_b = spread(low_b)
    purified = cube_part(*cube_jobs, right_a, right_b, square_a, square_b, pieces_a, pieces_b)
    return purified.reshape(own_rows, 1, 4, 128, 128)


def solution(mesh):
    axes = ("y", "z_lo", "z_hi", "x", "core")
    fine = Mesh(mesh.devices.reshape(4, 2, 4, 4, 2), axes)
    rows = ("y", "z_lo", "z_hi")
    return jax.shard_map(
        on_device,
        mesh=fine,
        in_specs=(P(rows, None, None, None), P(), P(rows, None, None)),
        out_specs=P(rows, ("x", "core"), None, None, None),
        check_vma=False,
    )
```

time: 620 us -> 295 us (0.48)
  waiting for transfers between devices: 455 us -> 209 us
  local copies, waits for them, and re-layouts: 83.5 us -> 12.5 us
  matrix products: 32.2 us -> 0 us
  starting transfers between devices: 0.04 us -> 31.3 us
  Pallas kernels: 0 us -> 21.7 us
  loops' own time: 15.8 us -> 0 us
  other arithmetic: 19.6 us -> 5.47 us
    all_gather x2, waiting for transfers between devices: 455 us -> 186 us  [the longest x1 96.9 us: on_device(): right_a = lax.all_gather(own_a, ('y', 'z_hi', 'z_lo'), axis=0, tiled=True)]
    gather x24 -> x0, local copies, waits for them, and re-layouts: 69.7 us -> none  [the longest x8 61.1 us: row_block(): b_tiles = jnp.take(column, index_part, axis=0)]
    dot_general x8 -> x0, matrix products: 32.2 us -> none  [row_block(): jnp.einsum('imab,imbc->imac', left_part, b_tiles, preferred_element_type=...]
    ppermute x0 -> x18, starting transfers between devices: none -> 31.3 us  [the longest x10 19.8 us: to_other_core(): return lax.ppermute(block, 'core', [(0, 1), (1, 0)])]
    pallas_call x0 -> x3, Pallas kernels: none -> 21.7 us  [the longest x1 12.5 us: cube_part(): pl.pallas_call(cube_kernel, out_shape=jax.ShapeDtypeStruct((64, 128, 128)...]
    ppermute x0 -> x18, waiting for transfers between devices: none -> 21.7 us  [the longest x8 19 us: along_x(): return lax.ppermute(block, 'x', [(i, (i + step) % 4) for i in range(4)])]
    another operation x2 -> x0, loops' own time: 15.8 us -> none  [filtered_product(): blocks = lax.map(row_block, starts)]
    convert_element_type x2, other arithmetic: 9.65 us -> 0.01 us  [packed_jobs(): hits = matched.astype(jnp.int32)]
  transfers between devices with their start and end apart: 2 -> 20, of which waited for: 2 -> 8; matrix products, arithmetic and copies ran while one was open for 0% -> 4% of each run, Pallas kernels for 0% -> 3%
where the time goes in v1:
time: 295 us; the launch traced here: 293 us
  waiting for transfers between devices  209 us (71%)
  starting transfers between devices  31.3 us (11%)
  Pallas kernels  21.7 us (7%)
  between operations  13.6 us (5%)
  local copies, waits for them, and re-layouts  12.5 us (4%)
  other arithmetic  5.47 us (2%)
    all_gather x1, waiting for transfers between devices, on_device(): right_a = lax.all_gather(own_a, ('y', 'z_hi', 'z_lo'), axis=0, tiled=True)  96.9 us
    all_gather x1, waiting for transfers between devices, on_device(): right_b = lax.all_gather(own_b, ('y', 'z_hi', 'z_lo'), axis=0, tiled=True)  89.4 us
    ppermute x10, starting transfers between devices, to_other_core(): return lax.ppermute(block, 'core', [(0, 1), (1, 0)])  19.8 us
    ppermute x8, waiting for transfers between devices, along_x(): return lax.ppermute(block, 'x', [(i, (i + step) % 4) for i in range(4)])  19 us
    pallas_call x1, Pallas kernels, cube_part(): pl.pallas_call(cube_kernel, out_shape=jax.ShapeDtypeStruct((64, 128, 128)...  12.5 us
    ppermute x8, starting transfers between devices, along_x(): return lax.ppermute(block, 'x', [(i, (i + step) % 4) for i in range(4)])  11.4 us
    pallas_call x2, Pallas kernels, square_part(): pl.pallas_call(square_kernel, out_shape=(jax.ShapeDtypeStruct((64, part,...  9.26 us
  transfers between devices with their start and end apart: 20, of which 8 were waited for; matrix products, arithmetic and copies ran while one was open for 4% of the time, Pallas kernels for 3%

profile of v1, /device:TPU:1, one launch (start us, length us, event | category | flops | bytes accessed | tf_op | source)
XLA Modules:
  0.0 293.3 jit_solution(2492167044171964719)
XLA Ops:
  6.5 1.1 constant_dynamic-slice_fusion.1
  7.6 0.3 copy.29
  7.9 0.8 fusion.31
  8.8 0.7 all-gather.5.cloned.1.call-update
  9.5 0.8 constant_dynamic-slice_fusion
  10.4 0.7 constant_dynamic-slice_fusion.2
  11.1 0.4 select_reduce_fusion.3
  11.6 0.7 dynamic-slice_bitcast_fusion
  12.5 0.8 fusion.13
  13.4 0.7 convert_reduce_fusion.1
  14.3 0.6 compare_select_fusion.4.jobs
  15.0 96.9 %all-gather.3.cloned.1.call-done.right.refs_2_ = bf16[512,64,128]{2,1,0:T(8,128)(2,1)} async-done(((bf16[16,64,128]{2,1,0:T(8,128)(2,1)}), bf16[512,64,128]{2,1,0:T(8,128)(2,1)}) %all-gather.3.cloned.1.call-update) | async-done | bytes 8388624 | tf_op jit(solution)/shard_map/all_gather | solution.py:247
  111.9 4.6 %square_part.2 = (f32[64,64,128]{2,1,0:T(8,128)S(1)}, bf16[64,64,128]{2,1,0:T(8,128)(2,1)S(1)}) custom-call(s32[128]{0:T(128)S(1)} %compare_select_fusion.4.jobs, s32[1]{0:T(128)} %bitcast.7.count, bf16[128,128,128]{2,1,0:T(8,128)(2,1)} %bitcast.13, bf16[512,64,128]{2,1,0:T(8,128)(2,1)} %all-gather.3.cloned.1.call-done.right.refs_2_), custom_call_target="tpu_custom_call" | custom-call | tf_op jit(solution)/shard_map/square_part/pallas_call | solution.py:59
  116.5 1.3 copy-done
  117.8 2.7 collective-permute-start.1
  120.5 89.4 %all-gather.5.cloned.1.call-done.right.refs_3_ = bf16[512,64,128]{2,1,0:T(8,128)(2,1)} async-done(((bf16[16,64,128]{2,1,0:T(8,128)(2,1)}), bf16[512,64,128]{2,1,0:T(8,128)(2,1)}) %all-gather.5.cloned.1.call-update) | async-done | bytes 8388624 | tf_op jit(solution)/shard_map/all_gather | solution.py:248
  209.9 4.7 %square_part.3 = (f32[64,64,128]{2,1,0:T(8,128)S(1)}, bf16[64,64,128]{2,1,0:T(8,128)(2,1)S(1)}) custom-call(s32[128]{0:T(128)S(1)} %compare_select_fusion.4.jobs, s32[1]{0:T(128)} %bitcast.7.count, bf16[128,128,128]{2,1,0:T(8,128)(2,1)} %bitcast.14, bf16[512,64,128]{2,1,0:T(8,128)(2,1)} %all-gather.5.cloned.1.call-done.right.refs_3_), custom_call_target="tpu_custom_call" | custom-call | tf_op jit(solution)/shard_map/square_part/pallas_call | solution.py:59
  214.6 1.3 copy-done.1
  215.9 2.7 collective-permute-start.10
  218.6 1.4 collective-permute-start.4
  220.1 0.9 copy-done.3
  221.0 3.0 %collective-permute-start.3 = (bf16[32,64,128]{2,1,0:T(8,128)(2,1)S(1)}, bf16[32,64,128]{2,1,0:T(8,128)(2,1)S(1)}, u32[]{:S(2)}, u32[]{:S(2)}) collective-permute-start(bf16[32,64,128]{2,1,0:T(8,128)(2,1)S(1)} %slice.27), channel_id=1, source_target_pairs={{0,6},{2,0},{4,2},{6,4},{1,7},{3,1},{5,3},{7,5},{8,14},{10,8},{12,... | collective-permute-start | bytes 1572872 | tf_op jit(solution)/shard_map/ppermute | solution.py:229
  224.0 1.9 slice.26
  225.9 14.1 %collective-permute-done.10.refs_18_ = bf16[64,64,128]{2,1,0:T(8,128)(2,1)S(1)} collective-permute-done((bf16[64,64,128]{2,1,0:T(8,128)(2,1)S(1)}, bf16[64,64,128]{2,1,0:T(8,128)(2,1)S(1)}, u32[]{:S(2)}, u32[]{:S(2)}) %collective-permute-start.10) | collective-permute-done | bytes 1048608 | tf_op jit(solution)/shard_map/ppermute | solution.py:229
  240.0 1.6 collective-permute-start.2
  241.5 0.8 slice.29
  242.4 0.7 collective-permute-done.9.refs_17_
  243.1 1.2 collective-permute-start.12
  244.3 0.8 slice.28
  245.1 0.3 collective-permute-start.11
  245.4 3.8 %collective-permute-start.6 = (bf16[64,64,128]{2,1,0:T(8,128)(2,1)}, bf16[64,64,128]{2,1,0:T(8,128)(2,1)}, u32[]{:S(2)}, u32[]{:S(2)}) collective-permute-start(bf16[64,64,128]{2,1,0:T(8,128)(2,1)} %copy-done.3), channel_id=1, source_target_pairs={{0,1},{1,0},{2,3},{3,2},{4,5},{5,4},{6,7},{7,6},{8,9},{9,8},{10,11... | collective-permute-start | bytes 3145736 | tf_op jit(solution)/shard_map/ppermute | solution.py:232
  249.2 2.0 collective-permute-done.3.refs_10_
  251.2 3.7 %collective-permute-start.8 = (bf16[32,64,128]{2,1,0:T(8,128)(2,1)S(1)}, bf16[32,64,128]{2,1,0:T(8,128)(2,1)}, u32[]{:S(2)}, u32[]{:S(2)}) collective-permute-start(bf16[32,64,128]{2,1,0:T(8,128)(2,1)S(1)} %collective-permute-done.3.refs_10_), channel_id=1, source_target_pairs={{0,1},{1,0},{2,3},{3,2},{4,5},{5,4},{6,7},{7,6},{8,9},{9,8},{10,11... | collective-permute-start | bytes 1572872 | tf_op jit(solution)/shard_map/ppermute | solution.py:232
  255.0 0.5 select_reduce_fusion.2
  255.6 4.8 %collective-permute-start.5 = (bf16[64,64,128]{2,1,0:T(8,128)(2,1)}, bf16[64,64,128]{2,1,0:T(8,128)(2,1)}, u32[]{:S(2)}, u32[]{:S(2)}) collective-permute-start(bf16[64,64,128]{2,1,0:T(8,128)(2,1)} %collective-permute-done.refs_7_), channel_id=1, source_target_pairs={{0,1},{1,0},{2,3},{3,2},{4,5},{5,4},{6,7},{7,6},{8,9},{9,8},{10,11... | collective-permute-start | bytes 3145736 | tf_op jit(solution)/shard_map/ppermute | solution.py:232
  260.4 2.2 collective-permute-done.12.refs_20_
  262.5 2.0 collective-permute-start.15
  264.6 3.4 %collective-permute-start.14 = (bf16[64,64,128]{2,1,0:T(8,128)(2,1)}, bf16[64,64,128]{2,1,0:T(8,128)(2,1)}, u32[]{:S(2)}, u32[]{:S(2)}) collective-permute-start(bf16[64,64,128]{2,1,0:T(8,128)(2,1)} %copy-done.5), channel_id=1, source_target_pairs={{0,1},{1,0},{2,3},{3,2},{4,5},{5,4},{6,7},{7,6},{8,9},{9,8},{10,11... | collective-permute-start | bytes 3145736 | tf_op jit(solution)/shard_map/ppermute | solution.py:232
  268.1 0.1 copy.28
  268.7 0.6 collective-permute-start.17
  269.2 2.5 collective-permute-done.7.refs_14_
  271.8 0.1 collective-permute-start.16
  271.9 0.7 convert_reduce_fusion
  272.7 0.1 select_reduce_fusion.1
  272.8 0.3 select_reduce_fusion
  273.1 0.7 fusion.26.refs_0_
  273.9 0.1 collective-permute-done.16.refs_24_
  274.0 12.5 %cube_part.1 = bf16[64,128,128]{2,1,0:T(8,128)(2,1)} custom-call(s32[512]{0:T(512)S(1)} %fusion.26.refs_0_, s32[1]{0:T(128)} %bitcast.3.refs_1_, bf16[512,64,128]{2,1,0:T(8,128)(2,1)} %all-gather.3.cloned.1.call-done.right.refs_2_, bf16[512,64,128]{2,1,0:T(8,128)(2,1)} %all-gather.5.cloned.1.call-done.right.refs_3_, f32[64,64,128]{2,1,0:T(8,128)} %copy-done, ...), custom_call_target="tpu_custom_call" | custom-call | tf_op jit(solution)/shard_map/cube_part/pallas_call | solution.py:156
  (63 shorter events, 1.9 us)
Async XLA Ops:
  6.5 105.3 %all-gather.3.cloned.1.call-start = ((), (), s32[]{:S(2)}) async-start(), calls=%async_computation | async-start | bytes 8650752 | tf_op jit(solution)/shard_map/all_gather | solution.py:247
  8.8 201.2 %all-gather.5.cloned.1.call-start = ((), (), s32[]{:S(2)}) async-start(), calls=%async_computation.1 | async-start | bytes 8650752 | tf_op jit(solution)/shard_map/all_gather | solution.py:248
  116.5 1.3 copy-start
  117.8 102.2 %collective-permute-start.1 = (bf16[64,64,128]{2,1,0:T(8,128)(2,1)S(1)}, bf16[64,64,128]{2,1,0:T(8,128)(2,1)S(1)}, u32[]{:S(2)}, u32[]{:S(2)}) collective-permute-start(bf16[64,64,128]{2,1,0:T(8,128)(2,1)S(1)} %get-tuple-element.11.refs_6_), channel_id=1, source_target_pairs={{0,6},{2,0},{4,2},{6,4},{1,7},{3,1},{5,3},{7,5},{8,14},{10,8},{12,... | collective-permute-start | bytes 3145736 | tf_op jit(solution)/shard_map/ppermute | solution.py:229
  120.5 100.5 %collective-permute-start = (bf16[64,64,128]{2,1,0:T(8,128)(2,1)S(1)}, bf16[64,64,128]{2,1,0:T(8,128)(2,1)}, u32[]{:S(2)}, u32[]{:S(2)}) collective-permute-start(bf16[64,64,128]{2,1,0:T(8,128)(2,1)S(1)} %get-tuple-element.11.refs_6_), channel_id=1, source_target_pairs={{0,2},{2,4},{4,6},{6,0},{1,3},{3,5},{5,7},{7,1},{8,10},{10,12},{12... | collective-permute-start | bytes 3145736 | tf_op jit(solution)/shard_map/ppermute | solution.py:229
  214.6 1.3 copy-start.1
  215.9 58.1 %copy-start.2 = (bf16[64,64,128]{2,1,0:T(8,128)(2,1)}, bf16[64,64,128]{2,1,0:T(8,128)(2,1)S(1)}, u32[]{:S(2)}) copy-start(bf16[64,64,128]{2,1,0:T(8,128)(2,1)S(1)} %get-tuple-element.12.refs_16_) | copy-start | bytes 3145732
  215.9 39.0 %copy-start.8 = (s32[16,8,4]{0,2,1:T(4,128)S(1)}, s32[16,8,4]{0,2,1:T(4,128)}, u32[]{:S(2)}) copy-start(s32[16,8,4]{0,2,1:T(4,128)} %param.5) | copy-start | bytes 6148
  215.9 24.1 %collective-permute-start.10 = (bf16[64,64,128]{2,1,0:T(8,128)(2,1)S(1)}, bf16[64,64,128]{2,1,0:T(8,128)(2,1)S(1)}, u32[]{:S(2)}, u32[]{:S(2)}) collective-permute-start(bf16[64,64,128]{2,1,0:T(8,128)(2,1)S(1)} %get-tuple-element.12.refs_16_), channel_id=1, source_target_pairs={{0,6},{2,0},{4,2},{6,4},{1,7},{3,1},{5,3},{7,5},{8,14},{10,8},{12,... | collective-permute-start | bytes 3145736 | tf_op jit(solution)/shard_map/ppermute | solution.py:229
  218.6 24.5 %collective-permute-start.9 = (bf16[64,64,128]{2,1,0:T(8,128)(2,1)S(1)}, bf16[64,64,128]{2,1,0:T(8,128)(2,1)S(1)}, u32[]{:S(2)}, u32[]{:S(2)}) collective-permute-start(bf16[64,64,128]{2,1,0:T(8,128)(2,1)S(1)} %get-tuple-element.12.refs_16_), channel_id=1, source_target_pairs={{0,2},{2,4},{4,6},{6,0},{1,3},{3,5},{5,7},{7,1},{8,10},{10,12},{12... | collective-permute-start | bytes 3145736 | tf_op jit(solution)/shard_map/ppermute | solution.py:229
  218.6 26.5 %collective-permute-start.4 = (bf16[64,64,128]{2,1,0:T(8,128)(2,1)S(1)}, bf16[64,64,128]{2,1,0:T(8,128)(2,1)S(1)}, u32[]{:S(2)}, u32[]{:S(2)}) collective-permute-start(bf16[64,64,128]{2,1,0:T(8,128)(2,1)S(1)} %get-tuple-element.11.refs_6_), channel_id=1, source_target_pairs={{0,1},{1,0},{2,3},{3,2},{4,5},{5,4},{6,7},{7,6},{8,9},{9,8},{10,11... | collective-permute-start | bytes 3145736 | tf_op jit(solution)/shard_map/ppermute | solution.py:232
  220.0 1.0 copy-start.3
  220.0 25.4 %collective-permute-start.13 = (bf16[64,64,128]{2,1,0:T(8,128)(2,1)S(1)}, bf16[64,64,128]{2,1,0:T(8,128)(2,1)S(1)}, u32[]{:S(2)}, u32[]{:S(2)}) collective-permute-start(bf16[64,64,128]{2,1,0:T(8,128)(2,1)S(1)} %get-tuple-element.12.refs_16_), channel_id=1, source_target_pairs={{0,1},{1,0},{2,3},{3,2},{4,5},{5,4},{6,7},{7,6},{8,9},{9,8},{10,11... | collective-permute-start | bytes 3145736 | tf_op jit(solution)/shard_map/ppermute | solution.py:232
  221.0 30.2 %collective-permute-start.3 = (bf16[32,64,128]{2,1,0:T(8,128)(2,1)S(1)}, bf16[32,64,128]{2,1,0:T(8,128)(2,1)S(1)}, u32[]{:S(2)}, u32[]{:S(2)}) collective-permute-start(bf16[32,64,128]{2,1,0:T(8,128)(2,1)S(1)} %slice.27), channel_id=1, source_target_pairs={{0,6},{2,0},{4,2},{6,4},{1,7},{3,1},{5,3},{7,5},{8,14},{10,8},{12,... | collective-permute-start | bytes 1572872 | tf_op jit(solution)/shard_map/ppermute | solution.py:229
  240.0 11.2 %copy-start.4 = (bf16[64,64,128]{2,1,0:T(8,128)(2,1)}, bf16[64,64,128]{2,1,0:T(8,128)(2,1)S(1)}, u32[]{:S(2)}) copy-start(bf16[64,64,128]{2,1,0:T(8,128)(2,1)S(1)} %collective-permute-done.10.refs_18_) | copy-start | bytes 3145732
  240.0 15.6 %collective-permute-start.2 = (bf16[32,64,128]{2,1,0:T(8,128)(2,1)}, bf16[32,64,128]{2,1,0:T(8,128)(2,1)S(1)}, u32[]{:S(2)}, u32[]{:S(2)}) collective-permute-start(bf16[32,64,128]{2,1,0:T(8,128)(2,1)} %slice.26), channel_id=1, source_target_pairs={{0,2},{2,4},{4,6},{6,0},{1,3},{3,5},{5,7},{7,1},{8,10},{10,12},{12... | collective-permute-start | bytes 1572872 | tf_op jit(solution)/shard_map/ppermute | solution.py:229
  243.1 11.8 %copy-start.5 = (bf16[64,64,128]{2,1,0:T(8,128)(2,1)}, bf16[64,64,128]{2,1,0:T(8,128)(2,1)S(1)}, u32[]{:S(2)}) copy-start(bf16[64,64,128]{2,1,0:T(8,128)(2,1)S(1)} %collective-permute-done.9.refs_17_) | copy-start | bytes 3145732
  243.1 19.4 %collective-permute-start.12 = (bf16[32,64,128]{2,1,0:T(8,128)(2,1)}, bf16[32,64,128]{2,1,0:T(8,128)(2,1)}, u32[]{:S(2)}, u32[]{:S(2)}) collective-permute-start(bf16[32,64,128]{2,1,0:T(8,128)(2,1)} %slice.29), channel_id=1, source_target_pairs={{0,6},{2,0},{4,2},{6,4},{1,7},{3,1},{5,3},{7,5},{8,14},{10,8},{12,... | collective-permute-start | bytes 1572872 | tf_op jit(solution)/shard_map/ppermute | solution.py:229
  245.1 9.8 %copy-start.6 = (bf16[64,64,128]{2,1,0:T(8,128)(2,1)}, bf16[64,64,128]{2,1,0:T(8,128)(2,1)S(1)}, u32[]{:S(2)}) copy-start(bf16[64,64,128]{2,1,0:T(8,128)(2,1)S(1)} %collective-permute-done.4.refs_11_) | copy-start | bytes 3145732
  245.1 19.4 %collective-permute-start.11 = (bf16[32,64,128]{2,1,0:T(8,128)(2,1)}, bf16[32,64,128]{2,1,0:T(8,128)(2,1)}, u32[]{:S(2)}, u32[]{:S(2)}) collective-permute-start(bf16[32,64,128]{2,1,0:T(8,128)(2,1)} %slice.28), channel_id=1, source_target_pairs={{0,2},{2,4},{4,6},{6,0},{1,3},{3,5},{5,7},{7,1},{8,10},{10,12},{12... | collective-permute-start | bytes 1572872 | tf_op jit(solution)/shard_map/ppermute | solution.py:229
  245.4 9.5 %copy-start.7 = (bf16[64,64,128]{2,1,0:T(8,128)(2,1)}, bf16[64,64,128]{2,1,0:T(8,128)(2,1)S(1)}, u32[]{:S(2)}) copy-start(bf16[64,64,128]{2,1,0:T(8,128)(2,1)S(1)} %collective-permute-done.13.refs_21_) | copy-start | bytes 3145732
  245.4 23.2 %collective-permute-start.6 = (bf16[64,64,128]{2,1,0:T(8,128)(2,1)}, bf16[64,64,128]{2,1,0:T(8,128)(2,1)}, u32[]{:S(2)}, u32[]{:S(2)}) collective-permute-start(bf16[64,64,128]{2,1,0:T(8,128)(2,1)} %copy-done.3), channel_id=1, source_target_pairs={{0,1},{1,0},{2,3},{3,2},{4,5},{5,4},{6,7},{7,6},{8,9},{9,8},{10,11... | collective-permute-start | bytes 3145736 | tf_op jit(solution)/shard_map/ppermute | solution.py:232
  251.2 16.8 %collective-permute-start.8 = (bf16[32,64,128]{2,1,0:T(8,128)(2,1)S(1)}, bf16[32,64,128]{2,1,0:T(8,128)(2,1)}, u32[]{:S(2)}, u32[]{:S(2)}) collective-permute-start(bf16[32,64,128]{2,1,0:T(8,128)(2,1)S(1)} %collective-permute-done.3.refs_10_), channel_id=1, source_target_pairs={{0,1},{1,0},{2,3},{3,2},{4,5},{5,4},{6,7},{7,6},{8,9},{9,8},{10,11... | collective-permute-start | bytes 1572872 | tf_op jit(solution)/shard_map/ppermute | solution.py:232
  255.6 18.2 %collective-permute-start.5 = (bf16[64,64,128]{2,1,0:T(8,128)(2,1)}, bf16[64,64,128]{2,1,0:T(8,128)(2,1)}, u32[]{:S(2)}, u32[]{:S(2)}) collective-permute-start(bf16[64,64,128]{2,1,0:T(8,128)(2,1)} %collective-permute-done.refs_7_), channel_id=1, source_target_pairs={{0,1},{1,0},{2,3},{3,2},{4,5},{5,4},{6,7},{7,6},{8,9},{9,8},{10,11... | collective-permute-start | bytes 3145736 | tf_op jit(solution)/shard_map/ppermute | solution.py:232
  262.5 11.3 %collective-permute-start.15 = (bf16[64,64,128]{2,1,0:T(8,128)(2,1)}, bf16[64,64,128]{2,1,0:T(8,128)(2,1)}, u32[]{:S(2)}, u32[]{:S(2)}) collective-permute-start(bf16[64,64,128]{2,1,0:T(8,128)(2,1)} %copy-done.4), channel_id=1, source_target_pairs={{0,1},{1,0},{2,3},{3,2},{4,5},{5,4},{6,7},{7,6},{8,9},{9,8},{10,11... | collective-permute-start | bytes 3145736 | tf_op jit(solution)/shard_map/ppermute | solution.py:232
  264.6 9.4 %collective-permute-start.14 = (bf16[64,64,128]{2,1,0:T(8,128)(2,1)}, bf16[64,64,128]{2,1,0:T(8,128)(2,1)}, u32[]{:S(2)}, u32[]{:S(2)}) collective-permute-start(bf16[64,64,128]{2,1,0:T(8,128)(2,1)} %copy-done.5), channel_id=1, source_target_pairs={{0,1},{1,0},{2,3},{3,2},{4,5},{5,4},{6,7},{7,6},{8,9},{9,8},{10,11... | collective-permute-start | bytes 3145736 | tf_op jit(solution)/shard_map/ppermute | solution.py:232
  268.0 3.8 %collective-permute-start.7 = (bf16[32,64,128]{2,1,0:T(8,128)(2,1)S(1)}, bf16[32,64,128]{2,1,0:T(8,128)(2,1)}, u32[]{:S(2)}, u32[]{:S(2)}) collective-permute-start(bf16[32,64,128]{2,1,0:T(8,128)(2,1)S(1)} %collective-permute-done.2.refs_9_), channel_id=1, source_target_pairs={{0,1},{1,0},{2,3},{3,2},{4,5},{5,4},{6,7},{7,6},{8,9},{9,8},{10,11... | collective-permute-start | bytes 1572872 | tf_op jit(solution)/shard_map/ppermute | solution.py:232
  268.7 5.2 %collective-permute-start.17 = (bf16[32,64,128]{2,1,0:T(8,128)(2,1)}, bf16[32,64,128]{2,1,0:T(8,128)(2,1)}, u32[]{:S(2)}, u32[]{:S(2)}) collective-permute-start(bf16[32,64,128]{2,1,0:T(8,128)(2,1)} %collective-permute-done.12.refs_20_), channel_id=1, source_target_pairs={{0,1},{1,0},{2,3},{3,2},{4,5},{5,4},{6,7},{7,6},{8,9},{9,8},{10,11... | collective-permute-start | bytes 1572872 | tf_op jit(solution)/shard_map/ppermute | solution.py:232
  271.8 2.3 collective-permute-start.16
Sparse Core Ops, SparseCore 0:
  9.9 101.8 all-gather.2
  114.5 95.3 all-gather.4
